TPU v7x, 128 devices: a whole 4x4x4 slice. The times are simulated.
128 devices in a mesh: row: 8 (over y, core), col: 16 (over z, x).
Axes of the slice: x: 4, y: 4, z: 4, core: 2. Of those that a mesh axis runs over, the one named last changes fastest.
Arguments:
- sigma_top: float32 [6144, 6144], P('row', 'col')
- factor_cross: float32 [6144, 6144], P('row', 'col'), may hold values from -0.078125 to 0.078125
- factor_inverse: float32 [6144, 6144], P('row', 'col')
- block_inverse: float32 [6144, 6144], P('row', 'col')
- ancestors: int32 [12], replicated, may hold values from 0 to 23, as said below
Outputs:
- sigma_cross: float32 [6144, 6144], P('row', 'col')
- sigma_child: float32 [6144, 6144], P('row', 'col')
Inputs may be any that keep to these rules, and one draw needn't show every extreme that they name: `ancestors`: 12 distinct block numbers; block 0 and block 23 are always among them.
All inputs are finite; a program needn't handle non-finite values.
Results may differ from a plain program's by a relative error of at most 0.000078.
Values sent between devices are 32-bit elements; how exact they have to be, the bound alone decides.
No kernel may reach another device: no remote copies, remote signals or barrier semaphores. Data moves between devices by JAX's collectives and lax.ppermute only.
A program may use at most 128 MiB of HBM per device.

v0:
```python
import jax
import jax.numpy as jnp
import numpy as np
from jax import lax
from jax.sharding import Mesh, PartitionSpec as P

NB = 24
NANC = 12
ROW = ("y", "core")
COL = ("z", "x")
ALL = ("y", "core", "z", "x")


def shift(x, axis, n, k):
    return lax.ppermute(x, axis, [(i, (i + k) % n) for i in range(n)])


def gather_rows(x):
    y, core = (lax.axis_index("y"), lax.axis_index("core"))
    half = x.shape[0] // 2
    left = shift(x, "y", 4, 1)
    right = shift(x, "y", 4, -1)
    far = jnp.concatenate([shift(left[:half], "y", 4, 1), shift(right[half:], "y", 4, -1)])
    mine = [x, left, right, far]
    at = [y, (y + 3) % 4, (y + 1) % 4, (y + 2) % 4]
    out = [(2 * a + core, t) for a, t in zip(at, mine)]
    out += [(2 * a + 1 - core, shift(t, "core", 2, 1)) for a, t in zip(at, mine)]
    return out


def spread(x):
    h, w = x.shape
    sub = h // 24
    return lax.all_to_all(x.reshape(3, 8, sub, w), ROW, 1, 0, tiled=True).reshape(NB, sub, w)


def pick(x, ancestors):
    return jnp.concatenate([lax.dynamic_slice_in_dim(x, ancestors[i], 1, 0) for i in range(NANC)])


def dot(a, b, dims):
    return lax.dot_general(
        a, b, (dims, ((), ())), precision=lax.Precision.HIGH, preferred_element_type=jnp.float32
    )


def per_device(sigma_top, factor_cross, factor_inverse, block_inverse, ancestors):
    h, w = sigma_top.shape
    sub = h // 24
    part = NANC * sub
    f = pick(spread(factor_cross), ancestors).reshape(part, w)
    f_all = lax.all_gather(f, COL, axis=1, tiled=True)
    strip = jnp.zeros((8 * h, w), jnp.float32)
    for r, t in gather_rows(factor_inverse):
        strip = lax.dynamic_update_slice(strip, t, (r * h, 0))
    s = pick(spread(sigma_top), ancestors).reshape(part, w)
    s_all = lax.all_gather(s, COL, axis=1, tiled=True)
    u = dot(f_all, strip, ((1,), (0,)))
    moved = lax.ppermute(
        u, ALL, [(16 * r + c, 16 * (c // 2) + 2 * r + c % 2) for r in range(8) for c in range(16)]
    )
    u_side = lax.all_gather(moved, COL, axis=0, tiled=False).reshape(8, 2, part, w)
    u_col = jnp.zeros((NANC, 8, sub, w), jnp.float32)
    for r, t in gather_rows(u):
        u_col = lax.dynamic_update_slice(u_col, t.reshape(NANC, 1, sub, w), (0, r, 0, 0))
    s_sel = jnp.concatenate(
        [lax.dynamic_slice_in_dim(s_all, ancestors[i] * 8 * sub, 8 * sub, 1) for i in range(NANC)],
        axis=1,
    )
    sigma = -dot(s_sel, u_col.reshape(8 * part, w), ((1,), (0,)))
    sigma_col = jnp.zeros((8, part, w), jnp.float32)
    for r, t in gather_rows(sigma):
        sigma_col = lax.dynamic_update_slice(sigma_col, t[None], (r, 0, 0))
    correction = jnp.concatenate([dot(u_side[:, p], sigma_col, ((0, 1), (0, 1))) for p in range(2)])
    sigma_child = block_inverse - correction
    blocks = sigma.reshape(NANC, sub, w)
    hit = ancestors[None, :] == lax.iota(jnp.int32, NB)[:, None]
    place = jnp.argmax(hit, axis=1)
    living = jnp.any(hit, axis=1)
    full = jnp.concatenate([lax.dynamic_slice_in_dim(blocks, place[b], 1, 0) for b in range(NB)])
    full = jnp.where(living[:, None, None], full, jnp.float32(0.0))
    back = lax.all_to_all(full.reshape(8, 3, sub, w), ROW, 0, 0, tiled=True)
    sigma_cross = back.reshape(8, 3, sub, w).transpose(1, 0, 2, 3).reshape(h, w)
    return (sigma_cross, sigma_child)


def solution(mesh):
    fine = Mesh(np.asarray(mesh.devices).reshape(4, 2, 4, 4), ALL)
    tile = P(ROW, COL)
    return jax.shard_map(
        per_device,
        mesh=fine,
        in_specs=(tile, tile, tile, tile, P()),
        out_specs=(tile, tile),
        check_vma=False,
    )
```

profile of v0, /device:TPU:1, one launch (start us, length us, event | category | flops | bytes accessed | tf_op | source)
XLA Modules:
  0.0 343.1 jit_solution(14482909959101323158)
XLA Ops:
  7.2 2.5 copy.63
  9.6 6.0 %all-to-all-start.1 = ((f32[3,8,32,384]{3,2,0,1:T(8,128)}), f32[3,8,32,384]{3,2,0,1:T(8,128)S(1)}, u32[]{:S(2)}, u32[]{:S(2)}) async-start(f32[3,8,32,384]{3,2,0,1:T(8,128)} %copy.63), calls=%async_computation.1 | async-start | bytes 2359296 | tf_op jit(solution)/shard_map/all_to_all | solution.py:34
  15.6 1.1 copy.62
  16.7 15.4 %all-to-all-done.1 = f32[3,8,32,384]{3,2,0,1:T(8,128)S(1)} async-done(((f32[3,8,32,384]{3,2,0,1:T(8,128)}), f32[3,8,32,384]{3,2,0,1:T(8,128)S(1)}, u32[]{:S(2)}, u32[]{:S(2)}) %all-to-all-start.1) | async-done | bytes 1179680 | tf_op jit(solution)/shard_map/all_to_all | solution.py:34
  32.1 4.3 %all-to-all-start = ((f32[3,8,32,384]{3,2,0,1:T(8,128)}), f32[3,8,32,384]{3,2,0,1:T(8,128)S(1)}, u32[]{:S(2)}, u32[]{:S(2)}) async-start(f32[3,8,32,384]{3,2,0,1:T(8,128)} %copy.62), calls=%async_computation | async-start | bytes 2359296 | tf_op jit(solution)/shard_map/all_to_all | solution.py:34
  61.3 1.5 collective-permute-start
  62.8 1.3 collective-permute-start.1
  64.1 26.1 %collective-permute-done = f32[768,384]{1,0:T(8,128)S(1)} collective-permute-done((f32[768,384]{1,0:T(8,128)}, f32[768,384]{1,0:T(8,128)S(1)}, u32[]{:S(2)}, u32[]{:S(2)}) %collective-permute-start) | collective-permute-done | bytes 1179680 | tf_op jit(solution)/shard_map/ppermute | solution.py:15
  90.4 2.7 collective-permute-start.3
  93.1 1.5 collective-permute-start.4
  95.2 10.4 %collective-permute-done.2 = f32[384,384]{1,0:T(8,128)S(1)} collective-permute-done((f32[384,384]{1,0:T(8,128)S(1)}, f32[384,384]{1,0:T(8,128)S(1)}, u32[]{:S(2)}, u32[]{:S(2)}) %collective-permute-start.2) | collective-permute-done | bytes 589856 | tf_op jit(solution)/shard_map/ppermute | solution.py:15
  105.6 1.8 collective-permute-start.7
  107.5 4.3 %broadcast_in_dim.53 = f32[6144,384]{1,0:T(8,128)} broadcast(f32[]{:T(128)} %constant.74.clone.1), dimensions={} | broadcast | bytes 9437188 | tf_op jit(solution)/shard_map/broadcast_in_dim | solution.py:53
  111.8 2.4 constant_dynamic-update-slice_fusion.69
  114.1 1.1 constant_dynamic-update-slice_fusion.68
  115.2 1.1 constant_dynamic-update-slice_fusion.67
  116.4 1.2 constant_dynamic-update-slice_fusion.66
  117.5 2.4 constant_dynamic-update-slice_fusion.65
  120.0 2.4 constant_dynamic-update-slice_fusion.64
  122.4 2.4 constant_dynamic-update-slice_fusion.63
  124.8 2.4 constant_dynamic-update-slice_fusion.62
  127.2 11.1 %all-gather.7.cloned.1.call-done = f32[384,6144]{1,0:T(8,128)} async-done(((f32[384,384]{1,0:T(8,128)}), f32[384,6144]{1,0:T(8,128)}) %all-gather.7.cloned.1.call-update) | async-done | bytes 9437200 | tf_op jit(solution)/shard_map/all_gather | solution.py:52
  138.3 11.7 %fusion.8 = f32[384,384]{1,0:T(8,128)S(1)} fusion(f32[384,6144]{1,0:T(8,128)} %all-gather.7.cloned.1.call-done, f32[6144,384]{1,0:T(8,128)} %constant_dynamic-update-slice_fusion.62), kind=kOutput, calls=%fused_computation.105 | convolution fusion | flops 5435817984 | bytes 19464192 | tf_op jit(solution)/shard_map/dot_general | solution.py:42
  150.0 5.2 %collective-permute-start.16 = (f32[384,384]{1,0:T(8,128)S(1)}, f32[384,384]{1,0:T(8,128)S(1)}, u32[]{:S(2)}, u32[]{:S(2)}) collective-permute-start(f32[384,384]{1,0:T(8,128)S(1)} %fusion.8), channel_id=1, source_target_pairs={{0,0},{1,1},{2,16},{3,17},{4,32},{5,33},{6,48},{7,49},{8,64},{9,65... | collective-permute-start | bytes 1769480 | tf_op jit(solution)/shard_map/ppermute | solution.py:59
  155.2 14.5 %collective-permute-done.16 = f32[384,384]{1,0:T(8,128)S(1)} collective-permute-done((f32[384,384]{1,0:T(8,128)S(1)}, f32[384,384]{1,0:T(8,128)S(1)}, u32[]{:S(2)}, u32[]{:S(2)}) %collective-permute-start.16) | collective-permute-done | bytes 589856 | tf_op jit(solution)/shard_map/ppermute | solution.py:59
  225.2 4.2 %collective-permute-start.8 = (f32[384,384]{1,0:T(8,128)S(1)}, f32[384,384]{1,0:T(8,128)S(1)}, u32[]{:S(2)}, u32[]{:S(2)}) collective-permute-start(f32[384,384]{1,0:T(8,128)S(1)} %fusion.8), channel_id=1, source_target_pairs={{0,32},{32,64},{64,96},{96,0},{1,33},{33,65},{65,97},{97,1},{2,34}... | collective-permute-start | bytes 1769480 | tf_op jit(solution)/shard_map/ppermute | solution.py:15
  229.4 4.4 %collective-permute-start.9 = (f32[384,384]{1,0:T(8,128)S(1)}, f32[384,384]{1,0:T(8,128)S(1)}, u32[]{:S(2)}, u32[]{:S(2)}) collective-permute-start(f32[384,384]{1,0:T(8,128)S(1)} %fusion.8), channel_id=1, source_target_pairs={{0,96},{32,0},{64,32},{96,64},{1,97},{33,1},{65,33},{97,65},{2,98}... | collective-permute-start | bytes 1769480 | tf_op jit(solution)/shard_map/ppermute | solution.py:15
  233.8 9.4 %collective-permute-start.12 = (f32[384,384]{1,0:T(8,128)S(1)}, f32[384,384]{1,0:T(8,128)S(1)}, u32[]{:S(2)}, u32[]{:S(2)}) collective-permute-start(f32[384,384]{1,0:T(8,128)S(1)} %fusion.8), channel_id=1, source_target_pairs={{0,16},{16,0},{1,17},{17,1},{2,18},{18,2},{3,19},{19,3},{4,20},{20... | collective-permute-start | bytes 1769480 | tf_op jit(solution)/shard_map/ppermute | solution.py:15
  255.5 2.7 collective-permute-start.11
  260.1 4.4 %collective-permute-done.10 = f32[192,384]{1,0:T(8,128)S(1)} collective-permute-done((f32[192,384]{1,0:T(8,128)S(1)}, f32[192,384]{1,0:T(8,128)S(1)}, u32[]{:S(2)}, u32[]{:S(2)}) %collective-permute-start.10) | collective-permute-done | bytes 294944 | tf_op jit(solution)/shard_map/ppermute | solution.py:15
  265.9 1.3 collective-permute-done.15
  267.3 2.5 broadcast_in_dim.55
  269.8 5.0 %bitcast_dynamic-update-slice_fusion.7 = (f32[8,384,384]{2,1,0:T(8,128)}, f32[384,384]{1,0:T(8,128)S(1)}) fusion(f32[8,384,384]{2,1,0:T(8,128)} %broadcast_in_dim.55, s32[]{:T(128)S(6)} %select_n.283, f32[384,3072]{1,0:T(8,128)S(1)} %dynamic-slice_dynamic-update-slice_fusion, f32[3072,384]{1,0:T(8,128)S(1)} %bitcast.119), kind=kOutput, calls=%fused_computation.15 | convolution fusion | flops 2718056448 | bytes 10616836 | tf_op jit(solution)/shard_map/dot_general | solution.py:42
  275.4 2.9 collective-permute-start.18
  279.4 1.2 broadcast_select_fusion
  280.5 3.5 %all-to-all-start.2 = ((f32[8,3,32,384]{3,2,1,0:T(8,128)}), f32[8,3,32,384]{3,2,1,0:T(8,128)S(1)}, u32[]{:S(2)}, u32[]{:S(2)}) async-start(f32[8,3,32,384]{3,2,1,0:T(8,128)} %broadcast_select_fusion), calls=%async_computation.2 | async-start | bytes 2359296 | tf_op jit(solution)/shard_map/all_to_all | solution.py:82
  284.0 7.7 %collective-permute-done.17 = f32[384,384]{1,0:T(8,128)S(1)} collective-permute-done((f32[384,384]{1,0:T(8,128)S(1)}, f32[384,384]{1,0:T(8,128)S(1)}, u32[]{:S(2)}, u32[]{:S(2)}) %collective-permute-start.17) | collective-permute-done | bytes 589856 | tf_op jit(solution)/shard_map/ppermute | solution.py:15
  292.0 3.7 %collective-permute-start.20 = (f32[192,384]{1,0:T(8,128)S(1)}, f32[192,384]{1,0:T(8,128)S(1)}, u32[]{:S(2)}, u32[]{:S(2)}) collective-permute-start(f32[192,384]{1,0:T(8,128)S(1)} %slice.206), channel_id=1, source_target_pairs={{0,96},{32,0},{64,32},{96,64},{1,97},{33,1},{65,33},{97,65},{2,98}... | collective-permute-start | bytes 884744 | tf_op jit(solution)/shard_map/ppermute | solution.py:15
  295.8 2.2 collective-permute-start.22
  299.6 11.1 %collective-permute-done.19 = f32[192,384]{1,0:T(8,128)S(1)} collective-permute-done((f32[192,384]{1,0:T(8,128)S(1)}, f32[192,384]{1,0:T(8,128)S(1)}, u32[]{:S(2)}, u32[]{:S(2)}) %collective-permute-start.19) | collective-permute-done | bytes 294944 | tf_op jit(solution)/shard_map/ppermute | solution.py:15
  312.7 1.9 bitcast_dynamic-update-slice_fusion.3
  314.6 1.1 copy.72
  315.7 1.9 bitcast_dynamic-update-slice_fusion.2
  317.6 1.9 bitcast_dynamic-update-slice_fusion.1
  319.6 1.9 bitcast_dynamic-update-slice_fusion
  321.5 7.8 %fusion.2 = f32[384,384]{1,0:T(8,128)S(1)} fusion(f32[8,384,384]{2,1,0:T(8,128)} %bitcast_dynamic-update-slice_fusion, f32[8,2,384,384]{3,2,1,0:T(8,128)} %bitcast.120), kind=kOutput, calls=%fused_computation.4 | convolution fusion | flops 2717908992 | bytes 10027008 | tf_op jit(solution)/shard_map/dot_general | solution.py:42
  329.3 6.1 %fusion.3 = f32[384,384]{1,0:T(8,128)S(1)} fusion(f32[8,384,384]{2,1,0:T(8,128)} %bitcast_dynamic-update-slice_fusion, f32[8,2,384,384]{3,2,1,0:T(8,128)S(1)} %bitcast.121), kind=kOutput, calls=%fused_computation.5 | convolution fusion | flops 2717908992 | bytes 10027008 | tf_op jit(solution)/shard_map/dot_general | solution.py:42
  335.4 1.1 maximum_subtract_fusion
  (143 shorter events, 27.5 us)
Async XLA Ops:
  7.2 8.4 %copy-start.2 = (f32[768,384]{1,0:T(8,128)S(1)}, f32[768,384]{1,0:T(8,128)}, u32[]{:S(2)}) copy-start(f32[768,384]{1,0:T(8,128)} %param.5) | copy-start | bytes 3538948
  7.2 29.3 %copy-start.6 = (s32[12]{0:T(128)S(1)}, s32[12]{0:T(128)}, u32[]{:S(2)}) copy-start(s32[12]{0:T(128)} %param.9) | copy-start | bytes 148
  9.6 22.5 %all-to-all-start.1 = ((f32[3,8,32,384]{3,2,0,1:T(8,128)}), f32[3,8,32,384]{3,2,0,1:T(8,128)S(1)}, u32[]{:S(2)}, u32[]{:S(2)}) async-start(f32[3,8,32,384]{3,2,0,1:T(8,128)} %copy.63), calls=%async_computation.1 | async-start | bytes 2359296 | tf_op jit(solution)/shard_map/all_to_all | solution.py:34
  32.1 26.9 %all-to-all-start = ((f32[3,8,32,384]{3,2,0,1:T(8,128)}), f32[3,8,32,384]{3,2,0,1:T(8,128)S(1)}, u32[]{:S(2)}, u32[]{:S(2)}) async-start(f32[3,8,32,384]{3,2,0,1:T(8,128)} %copy.62), calls=%async_computation | async-start | bytes 2359296 | tf_op jit(solution)/shard_map/all_to_all | solution.py:34
  36.5 101.8 %all-gather.7.cloned.1.call-start = ((), (), s32[]{:S(2)}) async-start(), calls=%async_computation.4 | async-start | bytes 10027008 | tf_op jit(solution)/shard_map/all_gather | solution.py:52
  59.3 0.8 copy-start.4
  60.2 183.0 %all-gather.5.cloned.1.call-start = ((), (), s32[]{:S(2)}) async-start(), calls=%async_computation.3 | async-start | bytes 10027008 | tf_op jit(solution)/shard_map/all_gather | solution.py:57
  60.4 0.8 copy-start.3
  61.3 260.2 %all-gather.9.cloned.1.call-start = ((), (), s32[]{:S(2)}) async-start(), calls=%async_computation.5 | async-start | bytes 10027008 | tf_op jit(solution)/shard_map/all_gather | solution.py:62
  61.3 28.9 %collective-permute-start = (f32[768,384]{1,0:T(8,128)}, f32[768,384]{1,0:T(8,128)S(1)}, u32[]{:S(2)}, u32[]{:S(2)}) collective-permute-start(f32[768,384]{1,0:T(8,128)} %param.7), channel_id=1, source_target_pairs={{0,32},{32,64},{64,96},{96,0},{1,33},{33,65},{65,97},{97,1},{2,34}... | collective-permute-start | bytes 3538952 | tf_op jit(solution)/shard_map/ppermute | solution.py:15
  62.8 27.6 %collective-permute-start.1 = (f32[768,384]{1,0:T(8,128)}, f32[768,384]{1,0:T(8,128)S(1)}, u32[]{:S(2)}, u32[]{:S(2)}) collective-permute-start(f32[768,384]{1,0:T(8,128)} %param.7), channel_id=1, source_target_pairs={{0,96},{32,0},{64,32},{96,64},{1,97},{33,1},{65,33},{97,65},{2,98}... | collective-permute-start | bytes 3538952 | tf_op jit(solution)/shard_map/ppermute | solution.py:15
  90.3 15.3 %collective-permute-start.2 = (f32[384,384]{1,0:T(8,128)S(1)}, f32[384,384]{1,0:T(8,128)S(1)}, u32[]{:S(2)}, u32[]{:S(2)}) collective-permute-start(f32[384,384]{1,0:T(8,128)S(1)} %slice.200), channel_id=1, source_target_pairs={{0,32},{32,64},{64,96},{96,0},{1,33},{33,65},{65,97},{97,1},{2,34}... | collective-permute-start | bytes 1769480 | tf_op jit(solution)/shard_map/ppermute | solution.py:15
  90.4 15.2 %collective-permute-start.3 = (f32[384,384]{1,0:T(8,128)S(1)}, f32[384,384]{1,0:T(8,128)S(1)}, u32[]{:S(2)}, u32[]{:S(2)}) collective-permute-start(f32[384,384]{1,0:T(8,128)S(1)} %slice.201), channel_id=1, source_target_pairs={{0,96},{32,0},{64,32},{96,64},{1,97},{33,1},{65,33},{97,65},{2,98}... | collective-permute-start | bytes 1769480 | tf_op jit(solution)/shard_map/ppermute | solution.py:15
  93.1 24.4 %collective-permute-start.4 = (f32[768,384]{1,0:T(8,128)}, f32[768,384]{1,0:T(8,128)}, u32[]{:S(2)}, u32[]{:S(2)}) collective-permute-start(f32[768,384]{1,0:T(8,128)} %param.7), channel_id=1, source_target_pairs={{0,16},{16,0},{1,17},{17,1},{2,18},{18,2},{3,19},{19,3},{4,20},{20... | collective-permute-start | bytes 3538952 | tf_op jit(solution)/shard_map/ppermute | solution.py:15
  94.7 25.3 %collective-permute-start.5 = (f32[768,384]{1,0:T(8,128)S(1)}, f32[768,384]{1,0:T(8,128)}, u32[]{:S(2)}, u32[]{:S(2)}) collective-permute-start(f32[768,384]{1,0:T(8,128)S(1)} %collective-permute-done), channel_id=1, source_target_pairs={{0,16},{16,0},{1,17},{17,1},{2,18},{18,2},{3,19},{19,3},{4,20},{20... | collective-permute-start | bytes 3538952 | tf_op jit(solution)/shard_map/ppermute | solution.py:15
  94.7 27.7 %collective-permute-start.6 = (f32[768,384]{1,0:T(8,128)S(1)}, f32[768,384]{1,0:T(8,128)}, u32[]{:S(2)}, u32[]{:S(2)}) collective-permute-start(f32[768,384]{1,0:T(8,128)S(1)} %collective-permute-done.1), channel_id=1, source_target_pairs={{0,16},{16,0},{1,17},{17,1},{2,18},{18,2},{3,19},{19,3},{4,20},{20... | collective-permute-start | bytes 3538952 | tf_op jit(solution)/shard_map/ppermute | solution.py:15
  105.6 19.2 %collective-permute-start.7 = (f32[768,384]{1,0:T(8,128)S(1)}, f32[768,384]{1,0:T(8,128)}, u32[]{:S(2)}, u32[]{:S(2)}) collective-permute-start(f32[768,384]{1,0:T(8,128)S(1)} %constant_dynamic-update-slice_fusion.24), channel_id=1, source_target_pairs={{0,16},{16,0},{1,17},{17,1},{2,18},{18,2},{3,19},{19,3},{4,20},{20... | collective-permute-start | bytes 3538952 | tf_op jit(solution)/shard_map/ppermute | solution.py:15
  150.0 19.7 %collective-permute-start.16 = (f32[384,384]{1,0:T(8,128)S(1)}, f32[384,384]{1,0:T(8,128)S(1)}, u32[]{:S(2)}, u32[]{:S(2)}) collective-permute-start(f32[384,384]{1,0:T(8,128)S(1)} %fusion.8), channel_id=1, source_target_pairs={{0,0},{1,1},{2,16},{3,17},{4,32},{5,33},{6,48},{7,49},{8,64},{9,65... | collective-permute-start | bytes 1769480 | tf_op jit(solution)/shard_map/ppermute | solution.py:59
  169.6 0.8 copy-start.5
  225.2 29.1 %collective-permute-start.8 = (f32[384,384]{1,0:T(8,128)S(1)}, f32[384,384]{1,0:T(8,128)S(1)}, u32[]{:S(2)}, u32[]{:S(2)}) collective-permute-start(f32[384,384]{1,0:T(8,128)S(1)} %fusion.8), channel_id=1, source_target_pairs={{0,32},{32,64},{64,96},{96,0},{1,33},{33,65},{65,97},{97,1},{2,34}... | collective-permute-start | bytes 1769480 | tf_op jit(solution)/shard_map/ppermute | solution.py:15
  229.4 26.1 %collective-permute-start.9 = (f32[384,384]{1,0:T(8,128)S(1)}, f32[384,384]{1,0:T(8,128)S(1)}, u32[]{:S(2)}, u32[]{:S(2)}) collective-permute-start(f32[384,384]{1,0:T(8,128)S(1)} %fusion.8), channel_id=1, source_target_pairs={{0,96},{32,0},{64,32},{96,64},{1,97},{33,1},{65,33},{97,65},{2,98}... | collective-permute-start | bytes 1769480 | tf_op jit(solution)/shard_map/ppermute | solution.py:15
  233.8 32.0 %collective-permute-start.12 = (f32[384,384]{1,0:T(8,128)S(1)}, f32[384,384]{1,0:T(8,128)S(1)}, u32[]{:S(2)}, u32[]{:S(2)}) collective-permute-start(f32[384,384]{1,0:T(8,128)S(1)} %fusion.8), channel_id=1, source_target_pairs={{0,16},{16,0},{1,17},{17,1},{2,18},{18,2},{3,19},{19,3},{4,20},{20... | collective-permute-start | bytes 1769480 | tf_op jit(solution)/shard_map/ppermute | solution.py:15
  254.4 10.1 %collective-permute-start.10 = (f32[192,384]{1,0:T(8,128)S(1)}, f32[192,384]{1,0:T(8,128)S(1)}, u32[]{:S(2)}, u32[]{:S(2)}) collective-permute-start(f32[192,384]{1,0:T(8,128)S(1)} %slice.202), channel_id=1, source_target_pairs={{0,32},{32,64},{64,96},{96,0},{1,33},{33,65},{65,97},{97,1},{2,34}... | collective-permute-start | bytes 884744 | tf_op jit(solution)/shard_map/ppermute | solution.py:15
  255.5 8.9 %collective-permute-start.11 = (f32[192,384]{1,0:T(8,128)S(1)}, f32[192,384]{1,0:T(8,128)S(1)}, u32[]{:S(2)}, u32[]{:S(2)}) collective-permute-start(f32[192,384]{1,0:T(8,128)S(1)} %slice.203), channel_id=1, source_target_pairs={{0,96},{32,0},{64,32},{96,64},{1,97},{33,1},{65,33},{97,65},{2,98}... | collective-permute-start | bytes 884744 | tf_op jit(solution)/shard_map/ppermute | solution.py:15
  259.3 6.5 %collective-permute-start.13 = (f32[384,384]{1,0:T(8,128)S(1)}, f32[384,384]{1,0:T(8,128)S(1)}, u32[]{:S(2)}, u32[]{:S(2)}) collective-permute-start(f32[384,384]{1,0:T(8,128)S(1)} %collective-permute-done.8), channel_id=1, source_target_pairs={{0,16},{16,0},{1,17},{17,1},{2,18},{18,2},{3,19},{19,3},{4,20},{20... | collective-permute-start | bytes 1769480 | tf_op jit(solution)/shard_map/ppermute | solution.py:15
  259.9 6.0 %collective-permute-start.14 = (f32[384,384]{1,0:T(8,128)S(1)}, f32[384,384]{1,0:T(8,128)S(1)}, u32[]{:S(2)}, u32[]{:S(2)}) collective-permute-start(f32[384,384]{1,0:T(8,128)S(1)} %collective-permute-done.9), channel_id=1, source_target_pairs={{0,16},{16,0},{1,17},{17,1},{2,18},{18,2},{3,19},{19,3},{4,20},{20... | collective-permute-start | bytes 1769480 | tf_op jit(solution)/shard_map/ppermute | solution.py:15
  264.5 2.7 collective-permute-start.15
  274.9 16.9 %collective-permute-start.17 = (f32[384,384]{1,0:T(8,128)S(1)}, f32[384,384]{1,0:T(8,128)S(1)}, u32[]{:S(2)}, u32[]{:S(2)}) collective-permute-start(f32[384,384]{1,0:T(8,128)S(1)} %get-tuple-element.41), channel_id=1, source_target_pairs={{0,32},{32,64},{64,96},{96,0},{1,33},{33,65},{65,97},{97,1},{2,34}... | collective-permute-start | bytes 1769480 | tf_op jit(solution)/shard_map/ppermute | solution.py:15
  275.4 16.7 %collective-permute-start.18 = (f32[384,384]{1,0:T(8,128)S(1)}, f32[384,384]{1,0:T(8,128)S(1)}, u32[]{:S(2)}, u32[]{:S(2)}) collective-permute-start(f32[384,384]{1,0:T(8,128)S(1)} %get-tuple-element.41), channel_id=1, source_target_pairs={{0,96},{32,0},{64,32},{96,64},{1,97},{33,1},{65,33},{97,65},{2,98}... | collective-permute-start | bytes 1769480 | tf_op jit(solution)/shard_map/ppermute | solution.py:15
  278.2 34.5 %collective-permute-start.21 = (f32[384,384]{1,0:T(8,128)S(1)}, f32[384,384]{1,0:T(8,128)}, u32[]{:S(2)}, u32[]{:S(2)}) collective-permute-start(f32[384,384]{1,0:T(8,128)S(1)} %get-tuple-element.41), channel_id=1, source_target_pairs={{0,16},{16,0},{1,17},{17,1},{2,18},{18,2},{3,19},{19,3},{4,20},{20... | collective-permute-start | bytes 1769480 | tf_op jit(solution)/shard_map/ppermute | solution.py:15
  280.5 34.1 %all-to-all-start.2 = ((f32[8,3,32,384]{3,2,1,0:T(8,128)}), f32[8,3,32,384]{3,2,1,0:T(8,128)S(1)}, u32[]{:S(2)}, u32[]{:S(2)}) async-start(f32[8,3,32,384]{3,2,1,0:T(8,128)} %broadcast_select_fusion), calls=%async_computation.2 | async-start | bytes 2359296 | tf_op jit(solution)/shard_map/all_to_all | solution.py:82
  291.8 18.9 %collective-permute-start.19 = (f32[192,384]{1,0:T(8,128)S(1)}, f32[192,384]{1,0:T(8,128)S(1)}, u32[]{:S(2)}, u32[]{:S(2)}) collective-permute-start(f32[192,384]{1,0:T(8,128)S(1)} %slice.205), channel_id=1, source_target_pairs={{0,32},{32,64},{64,96},{96,0},{1,33},{33,65},{65,97},{97,1},{2,34}... | collective-permute-start | bytes 884744 | tf_op jit(solution)/shard_map/ppermute | solution.py:15
  292.0 18.7 %collective-permute-start.20 = (f32[192,384]{1,0:T(8,128)S(1)}, f32[192,384]{1,0:T(8,128)S(1)}, u32[]{:S(2)}, u32[]{:S(2)}) collective-permute-start(f32[192,384]{1,0:T(8,128)S(1)} %slice.206), channel_id=1, source_target_pairs={{0,96},{32,0},{64,32},{96,64},{1,97},{33,1},{65,33},{97,65},{2,98}... | collective-permute-start | bytes 884744 | tf_op jit(solution)/shard_map/ppermute | solution.py:15
  295.8 20.0 %collective-permute-start.22 = (f32[384,384]{1,0:T(8,128)S(1)}, f32[384,384]{1,0:T(8,128)}, u32[]{:S(2)}, u32[]{:S(2)}) collective-permute-start(f32[384,384]{1,0:T(8,128)S(1)} %collective-permute-done.17), channel_id=1, source_target_pairs={{0,16},{16,0},{1,17},{17,1},{2,18},{18,2},{3,19},{19,3},{4,20},{20... | collective-permute-start | bytes 1769480 | tf_op jit(solution)/shard_map/ppermute | solution.py:15
  297.9 19.7 %collective-permute-start.23 = (f32[384,384]{1,0:T(8,128)S(1)}, f32[384,384]{1,0:T(8,128)}, u32[]{:S(2)}, u32[]{:S(2)}) collective-permute-start(f32[384,384]{1,0:T(8,128)S(1)} %collective-permute-done.18), channel_id=1, source_target_pairs={{0,16},{16,0},{1,17},{17,1},{2,18},{18,2},{3,19},{19,3},{4,20},{20... | collective-permute-start | bytes 1769480 | tf_op jit(solution)/shard_map/ppermute | solution.py:15
  310.8 8.8 %collective-permute-start.24 = (f32[384,384]{1,0:T(8,128)S(1)}, f32[384,384]{1,0:T(8,128)}, u32[]{:S(2)}, u32[]{:S(2)}) collective-permute-start(f32[384,384]{1,0:T(8,128)S(1)} %constant_dynamic-update-slice_fusion.52), channel_id=1, source_target_pairs={{0,16},{16,0},{1,17},{17,1},{2,18},{18,2},{3,19},{19,3},{4,20},{20... | collective-permute-start | bytes 1769480 | tf_op jit(solution)/shard_map/ppermute | solution.py:15
  321.5 7.8 %copy-start = (f32[6144,384]{1,0:T(8,128)S(1)}, f32[6144,384]{1,0:T(8,128)}, u32[]{:S(2)}) copy-start(f32[6144,384]{1,0:T(8,128)} %all-gather.9.cloned.1.call-done) | copy-start | bytes 28311556
  329.3 6.1 %copy-start.1 = (f32[768,384]{1,0:T(8,128)S(1)}, f32[768,384]{1,0:T(8,128)}, u32[]{:S(2)}) copy-start(f32[768,384]{1,0:T(8,128)} %param.8) | copy-start | bytes 3538948
Sparse Core Ops, SparseCore 0:
  60.3 77.9 all-gather.6
  141.0 100.0 all-gather.4
  243.3 75.4 all-gather.8
where the time goes:
time: 345 us; the launch traced here: 343 us
  waiting for transfers between devices  102 us (30%)
  between operations  89 us (26%)
  starting transfers between devices  62.1 us (18%)
  local copies, waits for them, and re-layouts  56.3 us (16%)
  matrix products  30.6 us (9%)
    ppermute x24, waiting for transfers between devices, shift(): return lax.ppermute(x, axis, [(i, (i + k) % n) for i in range(n)])  61.1 us
    ppermute x24, starting transfers between devices, shift(): return lax.ppermute(x, axis, [(i, (i + k) % n) for i in range(n)])  43.1 us
    dot_general x4, matrix products, dot(): lax.dot_general(a, b, (dims, ((), ())), precision=lax.Precision.HIGH, pre...  30.6 us
    dynamic_update_slice x8, local copies, waits for them, and re-layouts, per_device(): strip = lax.dynamic_update_slice(strip, t, (r * h, 0))  15.4 us
    all_to_all x2, waiting for transfers between devices, spread(): lax.all_to_all(x.reshape(3, 8, sub, w), ROW, 1, 0, tiled=True)  15.4 us
    unnamed x72, local copies, waits for them, and re-layouts  14.6 us
    ppermute x1, waiting for transfers between devices, per_device(): lax.ppermute(u, ALL, [(16 * r + c, 16 * (c // 2) + 2 * r + c % 2) for r i...  14.5 us
    all_gather x1, waiting for transfers between devices, per_device(): f_all = lax.all_gather(f, COL, axis=1, tiled=True)  11.1 us
  transfers between devices with their start and end apart: 31, of which 10 were waited for; matrix products, arithmetic and copies ran while one was open for 20% of the time, Pallas kernels for 0%

commit v1 on v0

--- a/solution.py
+++ b/solution.py
@@ -49,7 +49,9 @@
     sub = h // 24
     part = NANC * sub
     f = pick(spread(factor_cross), ancestors).reshape(part, w)
-    f_all = lax.all_gather(f, COL, axis=1, tiled=True)
+    built = jnp.stack([f for _ in range(jax.lax.psum(1, COL))], axis=0)
+    after = jax.lax.all_to_all(built, COL, 0, 0)
+    f_all = jnp.concatenate(after, 1)
     strip = jnp.zeros((8 * h, w), jnp.float32)
     for r, t in gather_rows(factor_inverse):
         strip = lax.dynamic_update_slice(strip, t, (r * h, 0))

time: 345 us -> 475 us (1.38)
  waiting for transfers between devices: 102 us -> 205 us
  local copies, waits for them, and re-layouts: 56.3 us -> 68.7 us
  starting transfers between devices: 62.1 us -> 73 us
    all_to_all x0 -> x1, waiting for transfers between devices: none -> 110 us  [per_device(): after = jax.lax.all_to_all(built, COL, 0, 0)]
    all_gather x1 -> x0, waiting for transfers between devices: 11.1 us -> none  [per_device(): f_all = lax.all_gather(f, COL, axis=1, tiled=True)]
    all_to_all x0 -> x1, starting transfers between devices: none -> 7.64 us  [per_device(): after = jax.lax.all_to_all(built, COL, 0, 0)]
    ppermute x24, waiting for transfers between devices: 61.1 us -> 68.7 us  [shift(): return lax.ppermute(x, axis, [(i, (i + k) % n) for i in range(n)])]
    dynamic_update_slice x8, local copies, waits for them, and re-layouts: 0.46 us -> 6.95 us  [per_device(): lax.dynamic_update_slice(u_col, t.reshape(NANC, 1, sub, w), (0, r, 0, 0))]
    ppermute x24, starting transfers between devices: 43.1 us -> 49.4 us  [shift(): return lax.ppermute(x, axis, [(i, (i + k) % n) for i in range(n)])]
    another operation x0 -> x2, local copies, waits for them, and re-layouts: none -> 4.8 us  [per_device(): built = jnp.stack([f for _ in range(jax.lax.psum(1, COL))], axis=0)]
    unnamed x72 -> x70, local copies, waits for them, and re-layouts: 14.6 us -> 13.7 us
  transfers between devices with their start and end apart: 31 -> 31, of which waited for: 10 -> 10; matrix products, arithmetic and copies ran while one was open for 20% -> 18% of each run, Pallas kernels for 0% -> 0%
where the time goes in v1:
time: 475 us; the launch traced here: 473 us
  waiting for transfers between devices  205 us (43%)
  between operations  90.3 us (19%)
  starting transfers between devices  73 us (15%)
  local copies, waits for them, and re-layouts  68.7 us (14%)
  matrix products  32.5 us (7%)
    all_to_all x1, waiting for transfers between devices, per_device(): after = jax.lax.all_to_all(built, COL, 0, 0)  110 us
    ppermute x24, waiting for transfers between devices, shift(): return lax.ppermute(x, axis, [(i, (i + k) % n) for i in range(n)])  68.7 us
    ppermute x24, starting transfers between devices, shift(): return lax.ppermute(x, axis, [(i, (i + k) % n) for i in range(n)])  49.4 us
    dot_general x4, matrix products, dot(): lax.dot_general(a, b, (dims, ((), ())), precision=lax.Precision.HIGH, pre...  32.5 us
    all_to_all x2, waiting for transfers between devices, spread(): lax.all_to_all(x.reshape(3, 8, sub, w), ROW, 1, 0, tiled=True)  15.4 us
    dynamic_update_slice x8, local copies, waits for them, and re-layouts, per_device(): strip = lax.dynamic_update_slice(strip, t, (r * h, 0))  15.2 us
    unnamed x70, local copies, waits for them, and re-layouts  13.7 us
    ppermute x1, waiting for transfers between devices, per_device(): lax.ppermute(u, ALL, [(16 * r + c, 16 * (c // 2) + 2 * r + c % 2) for r i...  10.8 us
  transfers between devices with their start and end apart: 31, of which 10 were waited for; matrix products, arithmetic and copies ran while one was open for 18% of the time, Pallas kernels for 0%

profile of v1, /device:TPU:1, one launch (start us, length us, event | category | flops | bytes accessed | tf_op | source)
XLA Modules:
  0.0 472.7 jit_solution(5567941563130105688)
XLA Ops:
  7.2 2.5 copy.67
  9.6 6.0 %all-to-all-start.1 = ((f32[3,8,32,384]{3,2,0,1:T(8,128)}), f32[3,8,32,384]{3,2,0,1:T(8,128)S(1)}, u32[]{:S(2)}, u32[]{:S(2)}) async-start(f32[3,8,32,384]{3,2,0,1:T(8,128)} %copy.67), calls=%async_computation.1 | async-start | bytes 2359296 | tf_op jit(solution)/shard_map/all_to_all | solution.py:34
  16.7 15.4 %all-to-all-done.1 = f32[3,8,32,384]{3,2,0,1:T(8,128)S(1)} async-done(((f32[3,8,32,384]{3,2,0,1:T(8,128)}), f32[3,8,32,384]{3,2,0,1:T(8,128)S(1)}, u32[]{:S(2)}, u32[]{:S(2)}) %all-to-all-start.1) | async-done | bytes 1179680 | tf_op jit(solution)/shard_map/all_to_all | solution.py:34
  32.1 4.3 all-to-all-start
  61.7 4.6 stack.3
  66.2 7.6 %all-to-all-start.2 = ((f32[16,384,384]{1,2,0:T(8,128)}), f32[16,384,384]{1,2,0:T(8,128)}, u32[]{:S(2)}, u32[]{:S(2)}) async-start(f32[16,384,384]{1,2,0:T(8,128)} %stack.3), calls=%async_computation.2 | async-start | bytes 18874368 | tf_op jit(solution)/shard_map/all_to_all | solution.py:53
  73.9 1.5 collective-permute-start
  75.4 1.3 collective-permute-start.1
  76.7 25.9 %collective-permute-done = f32[768,384]{1,0:T(8,128)S(1)} collective-permute-done((f32[768,384]{1,0:T(8,128)}, f32[768,384]{1,0:T(8,128)S(1)}, u32[]{:S(2)}, u32[]{:S(2)}) %collective-permute-start) | collective-permute-done | bytes 1179680 | tf_op jit(solution)/shard_map/ppermute | solution.py:15
  102.8 2.7 collective-permute-start.3
  105.6 1.7 collective-permute-start.4
  107.8 9.9 %collective-permute-done.2 = f32[384,384]{1,0:T(8,128)S(1)} collective-permute-done((f32[384,384]{1,0:T(8,128)S(1)}, f32[384,384]{1,0:T(8,128)S(1)}, u32[]{:S(2)}, u32[]{:S(2)}) %collective-permute-start.2) | collective-permute-done | bytes 589856 | tf_op jit(solution)/shard_map/ppermute | solution.py:15
  117.8 2.1 collective-permute-start.7
  119.9 4.3 broadcast_in_dim.53
  124.1 2.4 constant_dynamic-update-slice_fusion.69
  126.6 1.1 constant_dynamic-update-slice_fusion.68
  127.7 1.1 constant_dynamic-update-slice_fusion.67
  129.9 2.4 constant_dynamic-update-slice_fusion.65
  132.3 2.4 constant_dynamic-update-slice_fusion.64
  134.6 2.4 constant_dynamic-update-slice_fusion.63
  137.0 2.4 constant_dynamic-update-slice_fusion.62
  139.4 110.2 %all-to-all-done.2 = f32[16,384,384]{1,2,0:T(8,128)} async-done(((f32[16,384,384]{1,2,0:T(8,128)}), f32[16,384,384]{1,2,0:T(8,128)}, u32[]{:S(2)}, u32[]{:S(2)}) %all-to-all-start.2) | async-done | bytes 9437216 | tf_op jit(solution)/shard_map/all_to_all | solution.py:53
  249.6 11.5 %fusion.8 = f32[384,384]{1,0:T(8,128)S(1)} fusion(f32[384,6144]{0,1:T(8,128)} %bitcast.27, f32[6144,384]{1,0:T(8,128)} %constant_dynamic-update-slice_fusion.62), kind=kOutput, calls=%fused_computation.105 | convolution fusion | flops 5435817984 | bytes 19464192 | tf_op jit(solution)/shard_map/dot_general | solution.py:42
  261.2 1.9 collective-permute-start.16
  263.1 10.8 %collective-permute-done.16 = f32[384,384]{1,0:T(8,128)S(1)} collective-permute-done((f32[384,384]{1,0:T(8,128)S(1)}, f32[384,384]{1,0:T(8,128)S(1)}, u32[]{:S(2)}, u32[]{:S(2)}) %collective-permute-start.16) | collective-permute-done | bytes 589856 | tf_op jit(solution)/shard_map/ppermute | solution.py:61
  274.7 9.5 %collective-permute-start.8 = (f32[384,384]{1,0:T(8,128)S(1)}, f32[384,384]{1,0:T(8,128)S(1)}, u32[]{:S(2)}, u32[]{:S(2)}) collective-permute-start(f32[384,384]{1,0:T(8,128)S(1)} %fusion.8), channel_id=1, source_target_pairs={{0,32},{32,64},{64,96},{96,0},{1,33},{33,65},{65,97},{97,1},{2,34}... | collective-permute-start | bytes 1769480 | tf_op jit(solution)/shard_map/ppermute | solution.py:15
  284.2 2.1 collective-permute-start.9
  287.8 11.2 %collective-permute-done.8 = f32[384,384]{1,0:T(8,128)S(1)} collective-permute-done((f32[384,384]{1,0:T(8,128)S(1)}, f32[384,384]{1,0:T(8,128)S(1)}, u32[]{:S(2)}, u32[]{:S(2)}) %collective-permute-start.8) | collective-permute-done | bytes 589856 | tf_op jit(solution)/shard_map/ppermute | solution.py:15
  352.7 13.6 %collective-permute-start.12 = (f32[384,384]{1,0:T(8,128)S(1)}, f32[384,384]{1,0:T(8,128)S(1)}, u32[]{:S(2)}, u32[]{:S(2)}) collective-permute-start(f32[384,384]{1,0:T(8,128)S(1)} %fusion.8), channel_id=1, source_target_pairs={{0,16},{16,0},{1,17},{17,1},{2,18},{18,2},{3,19},{19,3},{4,20},{20... | collective-permute-start | bytes 1769480 | tf_op jit(solution)/shard_map/ppermute | solution.py:15
  366.3 3.0 collective-permute-start.11
  369.3 2.8 broadcast_in_dim.52
  374.3 1.4 collective-permute-done.11
  394.5 2.5 broadcast_in_dim.55
  397.0 7.1 %bitcast_dynamic-update-slice_fusion.7 = (f32[8,384,384]{2,1,0:T(8,128)}, f32[384,384]{1,0:T(8,128)S(1)}) fusion(f32[8,384,384]{2,1,0:T(8,128)} %broadcast_in_dim.55, s32[]{:T(128)S(6)} %select_n.283, f32[384,3072]{1,0:T(8,128)S(1)} %dynamic-slice_dynamic-update-slice_fusion, f32[3072,384]{1,0:T(8,128)} %bitcast.44), kind=kOutput, calls=%fused_computation.15 | convolution fusion | flops 2718056448 | bytes 10616836 | tf_op jit(solution)/shard_map/dot_general | solution.py:42
  404.1 3.4 collective-permute-start.18
  408.3 1.2 broadcast_select_fusion
  409.4 3.7 all-to-all-start.3
  413.1 8.1 %collective-permute-done.17 = f32[384,384]{1,0:T(8,128)S(1)} collective-permute-done((f32[384,384]{1,0:T(8,128)S(1)}, f32[384,384]{1,0:T(8,128)S(1)}, u32[]{:S(2)}, u32[]{:S(2)}) %collective-permute-start.17) | collective-permute-done | bytes 589856 | tf_op jit(solution)/shard_map/ppermute | solution.py:15
  421.7 3.6 collective-permute-start.20
  425.4 1.4 collective-permute-start.22
  428.5 11.7 %collective-permute-done.19 = f32[192,384]{1,0:T(8,128)S(1)} collective-permute-done((f32[192,384]{1,0:T(8,128)S(1)}, f32[192,384]{1,0:T(8,128)S(1)}, u32[]{:S(2)}, u32[]{:S(2)}) %collective-permute-start.19) | collective-permute-done | bytes 294944 | tf_op jit(solution)/shard_map/ppermute | solution.py:15
  442.0 1.9 bitcast_dynamic-update-slice_fusion.3
  445.0 1.9 bitcast_dynamic-update-slice_fusion.2
  446.9 1.9 bitcast_dynamic-update-slice_fusion.1
  448.9 1.9 bitcast_dynamic-update-slice_fusion
  450.8 7.8 %fusion.2 = f32[384,384]{1,0:T(8,128)S(1)} fusion(f32[8,384,384]{2,1,0:T(8,128)} %bitcast_dynamic-update-slice_fusion, f32[8,2,384,384]{3,2,1,0:T(8,128)} %bitcast.122), kind=kOutput, calls=%fused_computation.4 | convolution fusion | flops 2717908992 | bytes 10027008 | tf_op jit(solution)/shard_map/dot_general | solution.py:42
  458.6 6.1 %fusion.3 = f32[384,384]{1,0:T(8,128)S(1)} fusion(f32[8,384,384]{2,1,0:T(8,128)} %bitcast_dynamic-update-slice_fusion, f32[8,2,384,384]{3,2,1,0:T(8,128)S(1)} %bitcast.123), kind=kOutput, calls=%fused_computation.5 | convolution fusion | flops 2717908992 | bytes 10027008 | tf_op jit(solution)/shard_map/dot_general | solution.py:42
  464.7 1.1 maximum_subtract_fusion
  (142 shorter events, 35.0 us)
Async XLA Ops:
  7.2 8.4 %copy-start.2 = (f32[768,384]{1,0:T(8,128)S(1)}, f32[768,384]{1,0:T(8,128)}, u32[]{:S(2)}) copy-start(f32[768,384]{1,0:T(8,128)} %param.5) | copy-start | bytes 3538948
  7.2 29.3 %copy-start.5 = (s32[12]{0:T(128)S(1)}, s32[12]{0:T(128)}, u32[]{:S(2)}) copy-start(s32[12]{0:T(128)} %param.9) | copy-start | bytes 148
  9.6 22.5 %all-to-all-start.1 = ((f32[3,8,32,384]{3,2,0,1:T(8,128)}), f32[3,8,32,384]{3,2,0,1:T(8,128)S(1)}, u32[]{:S(2)}, u32[]{:S(2)}) async-start(f32[3,8,32,384]{3,2,0,1:T(8,128)} %copy.67), calls=%async_computation.1 | async-start | bytes 2359296 | tf_op jit(solution)/shard_map/all_to_all | solution.py:34
  32.1 28.0 %all-to-all-start = ((f32[3,8,32,384]{3,2,0,1:T(8,128)}), f32[3,8,32,384]{3,2,0,1:T(8,128)S(1)}, u32[]{:S(2)}, u32[]{:S(2)}) async-start(f32[3,8,32,384]{3,2,0,1:T(8,128)} %copy.66), calls=%async_computation | async-start | bytes 2359296 | tf_op jit(solution)/shard_map/all_to_all | solution.py:34
  36.5 345.5 %all-gather.4.cloned.1.call-start = ((), (), s32[]{:S(2)}) async-start(), calls=%async_computation.4 | async-start | bytes 10027008 | tf_op jit(solution)/shard_map/all_gather | solution.py:59
  60.4 0.8 copy-start.3
  66.2 183.4 %all-to-all-start.2 = ((f32[16,384,384]{1,2,0:T(8,128)}), f32[16,384,384]{1,2,0:T(8,128)}, u32[]{:S(2)}, u32[]{:S(2)}) async-start(f32[16,384,384]{1,2,0:T(8,128)} %stack.3), calls=%async_computation.2 | async-start | bytes 18874368 | tf_op jit(solution)/shard_map/all_to_all | solution.py:53
  73.9 376.9 %all-gather.6.cloned.1.call-start = ((), (), s32[]{:S(2)}) async-start(), calls=%async_computation.5 | async-start | bytes 10027008 | tf_op jit(solution)/shard_map/all_gather | solution.py:64
  73.9 28.7 %collective-permute-start = (f32[768,384]{1,0:T(8,128)}, f32[768,384]{1,0:T(8,128)S(1)}, u32[]{:S(2)}, u32[]{:S(2)}) collective-permute-start(f32[768,384]{1,0:T(8,128)} %param.7), channel_id=1, source_target_pairs={{0,32},{32,64},{64,96},{96,0},{1,33},{33,65},{65,97},{97,1},{2,34}... | collective-permute-start | bytes 3538952 | tf_op jit(solution)/shard_map/ppermute | solution.py:15
  75.4 27.4 %collective-permute-start.1 = (f32[768,384]{1,0:T(8,128)}, f32[768,384]{1,0:T(8,128)S(1)}, u32[]{:S(2)}, u32[]{:S(2)}) collective-permute-start(f32[768,384]{1,0:T(8,128)} %param.7), channel_id=1, source_target_pairs={{0,96},{32,0},{64,32},{96,64},{1,97},{33,1},{65,33},{97,65},{2,98}... | collective-permute-start | bytes 3538952 | tf_op jit(solution)/shard_map/ppermute | solution.py:15
  102.7 15.0 %collective-permute-start.2 = (f32[384,384]{1,0:T(8,128)S(1)}, f32[384,384]{1,0:T(8,128)S(1)}, u32[]{:S(2)}, u32[]{:S(2)}) collective-permute-start(f32[384,384]{1,0:T(8,128)S(1)} %slice.200), channel_id=1, source_target_pairs={{0,32},{32,64},{64,96},{96,0},{1,33},{33,65},{65,97},{97,1},{2,34}... | collective-permute-start | bytes 1769480 | tf_op jit(solution)/shard_map/ppermute | solution.py:15
  102.8 14.9 %collective-permute-start.3 = (f32[384,384]{1,0:T(8,128)S(1)}, f32[384,384]{1,0:T(8,128)S(1)}, u32[]{:S(2)}, u32[]{:S(2)}) collective-permute-start(f32[384,384]{1,0:T(8,128)S(1)} %slice.201), channel_id=1, source_target_pairs={{0,96},{32,0},{64,32},{96,64},{1,97},{33,1},{65,33},{97,65},{2,98}... | collective-permute-start | bytes 1769480 | tf_op jit(solution)/shard_map/ppermute | solution.py:15
  105.6 24.3 %collective-permute-start.4 = (f32[768,384]{1,0:T(8,128)}, f32[768,384]{1,0:T(8,128)}, u32[]{:S(2)}, u32[]{:S(2)}) collective-permute-start(f32[768,384]{1,0:T(8,128)} %param.7), channel_id=1, source_target_pairs={{0,16},{16,0},{1,17},{17,1},{2,18},{18,2},{3,19},{19,3},{4,20},{20... | collective-permute-start | bytes 3538952 | tf_op jit(solution)/shard_map/ppermute | solution.py:15
  107.3 25.0 %collective-permute-start.5 = (f32[768,384]{1,0:T(8,128)S(1)}, f32[768,384]{1,0:T(8,128)}, u32[]{:S(2)}, u32[]{:S(2)}) collective-permute-start(f32[768,384]{1,0:T(8,128)S(1)} %collective-permute-done), channel_id=1, source_target_pairs={{0,16},{16,0},{1,17},{17,1},{2,18},{18,2},{3,19},{19,3},{4,20},{20... | collective-permute-start | bytes 3538952 | tf_op jit(solution)/shard_map/ppermute | solution.py:15
  107.3 27.4 %collective-permute-start.6 = (f32[768,384]{1,0:T(8,128)S(1)}, f32[768,384]{1,0:T(8,128)}, u32[]{:S(2)}, u32[]{:S(2)}) collective-permute-start(f32[768,384]{1,0:T(8,128)S(1)} %collective-permute-done.1), channel_id=1, source_target_pairs={{0,16},{16,0},{1,17},{17,1},{2,18},{18,2},{3,19},{19,3},{4,20},{20... | collective-permute-start | bytes 3538952 | tf_op jit(solution)/shard_map/ppermute | solution.py:15
  117.8 19.2 %collective-permute-start.7 = (f32[768,384]{1,0:T(8,128)S(1)}, f32[768,384]{1,0:T(8,128)}, u32[]{:S(2)}, u32[]{:S(2)}) collective-permute-start(f32[768,384]{1,0:T(8,128)S(1)} %constant_dynamic-update-slice_fusion.24), channel_id=1, source_target_pairs={{0,16},{16,0},{1,17},{17,1},{2,18},{18,2},{3,19},{19,3},{4,20},{20... | collective-permute-start | bytes 3538952 | tf_op jit(solution)/shard_map/ppermute | solution.py:15
  261.2 12.7 %collective-permute-start.16 = (f32[384,384]{1,0:T(8,128)S(1)}, f32[384,384]{1,0:T(8,128)S(1)}, u32[]{:S(2)}, u32[]{:S(2)}) collective-permute-start(f32[384,384]{1,0:T(8,128)S(1)} %fusion.8), channel_id=1, source_target_pairs={{0,0},{1,1},{2,16},{3,17},{4,32},{5,33},{6,48},{7,49},{8,64},{9,65... | collective-permute-start | bytes 1769480 | tf_op jit(solution)/shard_map/ppermute | solution.py:61
  273.9 0.8 copy-start.4
  274.7 24.3 %collective-permute-start.8 = (f32[384,384]{1,0:T(8,128)S(1)}, f32[384,384]{1,0:T(8,128)S(1)}, u32[]{:S(2)}, u32[]{:S(2)}) collective-permute-start(f32[384,384]{1,0:T(8,128)S(1)} %fusion.8), channel_id=1, source_target_pairs={{0,32},{32,64},{64,96},{96,0},{1,33},{33,65},{65,97},{97,1},{2,34}... | collective-permute-start | bytes 1769480 | tf_op jit(solution)/shard_map/ppermute | solution.py:15
  284.2 82.2 %collective-permute-start.9 = (f32[384,384]{1,0:T(8,128)S(1)}, f32[384,384]{1,0:T(8,128)S(1)}, u32[]{:S(2)}, u32[]{:S(2)}) collective-permute-start(f32[384,384]{1,0:T(8,128)S(1)} %fusion.8), channel_id=1, source_target_pairs={{0,96},{32,0},{64,32},{96,64},{1,97},{33,1},{65,33},{97,65},{2,98}... | collective-permute-start | bytes 1769480 | tf_op jit(solution)/shard_map/ppermute | solution.py:15
  299.0 75.3 %collective-permute-start.10 = (f32[192,384]{1,0:T(8,128)S(1)}, f32[192,384]{1,0:T(8,128)S(1)}, u32[]{:S(2)}, u32[]{:S(2)}) collective-permute-start(f32[192,384]{1,0:T(8,128)S(1)} %slice.202), channel_id=1, source_target_pairs={{0,32},{32,64},{64,96},{96,0},{1,33},{33,65},{65,97},{97,1},{2,34}... | collective-permute-start | bytes 884744 | tf_op jit(solution)/shard_map/ppermute | solution.py:15
  352.7 25.8 %collective-permute-start.12 = (f32[384,384]{1,0:T(8,128)S(1)}, f32[384,384]{1,0:T(8,128)S(1)}, u32[]{:S(2)}, u32[]{:S(2)}) collective-permute-start(f32[384,384]{1,0:T(8,128)S(1)} %fusion.8), channel_id=1, source_target_pairs={{0,16},{16,0},{1,17},{17,1},{2,18},{18,2},{3,19},{19,3},{4,20},{20... | collective-permute-start | bytes 1769480 | tf_op jit(solution)/shard_map/ppermute | solution.py:15
  366.3 9.4 %collective-permute-start.11 = (f32[192,384]{1,0:T(8,128)S(1)}, f32[192,384]{1,0:T(8,128)S(1)}, u32[]{:S(2)}, u32[]{:S(2)}) collective-permute-start(f32[192,384]{1,0:T(8,128)S(1)} %slice.203), channel_id=1, source_target_pairs={{0,96},{32,0},{64,32},{96,64},{1,97},{33,1},{65,33},{97,65},{2,98}... | collective-permute-start | bytes 884744 | tf_op jit(solution)/shard_map/ppermute | solution.py:15
  372.9 6.4 %collective-permute-start.13 = (f32[384,384]{1,0:T(8,128)S(1)}, f32[384,384]{1,0:T(8,128)S(1)}, u32[]{:S(2)}, u32[]{:S(2)}) collective-permute-start(f32[384,384]{1,0:T(8,128)S(1)} %collective-permute-done.8), channel_id=1, source_target_pairs={{0,16},{16,0},{1,17},{17,1},{2,18},{18,2},{3,19},{19,3},{4,20},{20... | collective-permute-start | bytes 1769480 | tf_op jit(solution)/shard_map/ppermute | solution.py:15
  373.2 6.9 %collective-permute-start.14 = (f32[384,384]{1,0:T(8,128)S(1)}, f32[384,384]{1,0:T(8,128)S(1)}, u32[]{:S(2)}, u32[]{:S(2)}) collective-permute-start(f32[384,384]{1,0:T(8,128)S(1)} %collective-permute-done.9), channel_id=1, source_target_pairs={{0,16},{16,0},{1,17},{17,1},{2,18},{18,2},{3,19},{19,3},{4,20},{20... | collective-permute-start | bytes 1769480 | tf_op jit(solution)/shard_map/ppermute | solution.py:15
  375.8 5.2 %collective-permute-start.15 = (f32[384,384]{1,0:T(8,128)S(1)}, f32[384,384]{1,0:T(8,128)S(1)}, u32[]{:S(2)}, u32[]{:S(2)}) collective-permute-start(f32[384,384]{1,0:T(8,128)S(1)} %constant_dynamic-update-slice_fusion.26), channel_id=1, source_target_pairs={{0,16},{16,0},{1,17},{17,1},{2,18},{18,2},{3,19},{19,3},{4,20},{20... | collective-permute-start | bytes 1769480 | tf_op jit(solution)/shard_map/ppermute | solution.py:15
  404.1 17.1 %collective-permute-start.17 = (f32[384,384]{1,0:T(8,128)S(1)}, f32[384,384]{1,0:T(8,128)S(1)}, u32[]{:S(2)}, u32[]{:S(2)}) collective-permute-start(f32[384,384]{1,0:T(8,128)S(1)} %get-tuple-element.41), channel_id=1, source_target_pairs={{0,32},{32,64},{64,96},{96,0},{1,33},{33,65},{65,97},{97,1},{2,34}... | collective-permute-start | bytes 1769480 | tf_op jit(solution)/shard_map/ppermute | solution.py:15
  404.1 17.6 %collective-permute-start.18 = (f32[384,384]{1,0:T(8,128)S(1)}, f32[384,384]{1,0:T(8,128)S(1)}, u32[]{:S(2)}, u32[]{:S(2)}) collective-permute-start(f32[384,384]{1,0:T(8,128)S(1)} %get-tuple-element.41), channel_id=1, source_target_pairs={{0,96},{32,0},{64,32},{96,64},{1,97},{33,1},{65,33},{97,65},{2,98}... | collective-permute-start | bytes 1769480 | tf_op jit(solution)/shard_map/ppermute | solution.py:15
  407.5 34.5 %collective-permute-start.21 = (f32[384,384]{1,0:T(8,128)S(1)}, f32[384,384]{1,0:T(8,128)}, u32[]{:S(2)}, u32[]{:S(2)}) collective-permute-start(f32[384,384]{1,0:T(8,128)S(1)} %get-tuple-element.41), channel_id=1, source_target_pairs={{0,16},{16,0},{1,17},{17,1},{2,18},{18,2},{3,19},{19,3},{4,20},{20... | collective-permute-start | bytes 1769480 | tf_op jit(solution)/shard_map/ppermute | solution.py:15
  409.4 34.5 %all-to-all-start.3 = ((f32[8,3,32,384]{3,2,1,0:T(8,128)}), f32[8,3,32,384]{3,2,1,0:T(8,128)S(1)}, u32[]{:S(2)}, u32[]{:S(2)}) async-start(f32[8,3,32,384]{3,2,1,0:T(8,128)} %broadcast_select_fusion), calls=%async_computation.3 | async-start | bytes 2359296 | tf_op jit(solution)/shard_map/all_to_all | solution.py:84
  421.2 18.9 %collective-permute-start.19 = (f32[192,384]{1,0:T(8,128)S(1)}, f32[192,384]{1,0:T(8,128)S(1)}, u32[]{:S(2)}, u32[]{:S(2)}) collective-permute-start(f32[192,384]{1,0:T(8,128)S(1)} %slice.205), channel_id=1, source_target_pairs={{0,32},{32,64},{64,96},{96,0},{1,33},{33,65},{65,97},{97,1},{2,34}... | collective-permute-start | bytes 884744 | tf_op jit(solution)/shard_map/ppermute | solution.py:15
  421.7 18.5 %collective-permute-start.20 = (f32[192,384]{1,0:T(8,128)S(1)}, f32[192,384]{1,0:T(8,128)S(1)}, u32[]{:S(2)}, u32[]{:S(2)}) collective-permute-start(f32[192,384]{1,0:T(8,128)S(1)} %slice.206), channel_id=1, source_target_pairs={{0,96},{32,0},{64,32},{96,64},{1,97},{33,1},{65,33},{97,65},{2,98}... | collective-permute-start | bytes 884744 | tf_op jit(solution)/shard_map/ppermute | solution.py:15
  425.4 19.6 %collective-permute-start.22 = (f32[384,384]{1,0:T(8,128)S(1)}, f32[384,384]{1,0:T(8,128)}, u32[]{:S(2)}, u32[]{:S(2)}) collective-permute-start(f32[384,384]{1,0:T(8,128)S(1)} %collective-permute-done.17), channel_id=1, source_target_pairs={{0,16},{16,0},{1,17},{17,1},{2,18},{18,2},{3,19},{19,3},{4,20},{20... | collective-permute-start | bytes 1769480 | tf_op jit(solution)/shard_map/ppermute | solution.py:15
  426.8 20.1 %collective-permute-start.23 = (f32[384,384]{1,0:T(8,128)S(1)}, f32[384,384]{1,0:T(8,128)}, u32[]{:S(2)}, u32[]{:S(2)}) collective-permute-start(f32[384,384]{1,0:T(8,128)S(1)} %collective-permute-done.18), channel_id=1, source_target_pairs={{0,16},{16,0},{1,17},{17,1},{2,18},{18,2},{3,19},{19,3},{4,20},{20... | collective-permute-start | bytes 1769480 | tf_op jit(solution)/shard_map/ppermute | solution.py:15
  440.2 8.6 %collective-permute-start.24 = (f32[384,384]{1,0:T(8,128)S(1)}, f32[384,384]{1,0:T(8,128)}, u32[]{:S(2)}, u32[]{:S(2)}) collective-permute-start(f32[384,384]{1,0:T(8,128)S(1)} %constant_dynamic-update-slice_fusion.52), channel_id=1, source_target_pairs={{0,16},{16,0},{1,17},{17,1},{2,18},{18,2},{3,19},{19,3},{4,20},{20... | collective-permute-start | bytes 1769480 | tf_op jit(solution)/shard_map/ppermute | solution.py:15
  450.8 7.8 %copy-start = (f32[6144,384]{1,0:T(8,128)S(1)}, f32[6144,384]{1,0:T(8,128)}, u32[]{:S(2)}) copy-start(f32[6144,384]{1,0:T(8,128)} %all-gather.6.cloned.1.call-done) | copy-start | bytes 28311556
  458.6 6.1 %copy-start.1 = (f32[768,384]{1,0:T(8,128)S(1)}, f32[768,384]{1,0:T(8,128)}, u32[]{:S(2)}) copy-start(f32[768,384]{1,0:T(8,128)} %param.8) | copy-start | bytes 3538948
Sparse Core Ops, SparseCore 0:
  61.3 196.5 all-gather.3
  274.8 95.2 all-gather.5
